TPU v7x, 512 devices: a whole 4x4x16 slice. The times are simulated.
512 devices in a mesh: cell: 16 (over x, z_hi), hour: 8 (over z_lo, core), cat: 4 (over y).
Axes of the slice: x: 4, y: 4, z: 16 (z_hi: 4, z_lo: 4; z = z_hi * 4 + z_lo), core: 2. Of those that a mesh axis runs over, the one named last changes fastest.
Arguments:
- demand: bfloat16 [512, 128, 16384], P('hour', 'cat', 'cell'), may hold values from -16 to 16
- hour_factor: bfloat16 [512, 64], P(('hour', 'cell')), may hold values from -1 to 1, as said below
- cat_factor: bfloat16 [128, 64], P(('cat', 'cell')), may hold values from -1 to 1, as said below
Outputs:
- cell_factor: float32 [64, 16384], P(None, 'cell')
Inputs may be any that keep to these rules, and one draw needn't show every extreme that they name: `hour_factor`: factor entries; the largest magnitude is exactly 1. `cat_factor`: factor entries; the largest magnitude is exactly 1.
All inputs are finite; a program needn't handle non-finite values.
Results may differ from a plain program's by a relative error of at most 0.0029.
Values may be sent and summed in bfloat16 or wider, within the bound.
No kernel may reach another device: no remote copies, remote signals or barrier semaphores. Data moves between devices by JAX's collectives and lax.ppermute only.
A program may use at most 64 MiB of HBM per device.

v0:
```python
import jax
import jax.numpy as jnp
from jax import lax
from jax.sharding import PartitionSpec as P


def shards(demand, hour_factor, cat_factor):
    hour_rows, cat_rows = (
        lax.all_gather(hour_factor, "cell", axis=0, tiled=True),
        lax.all_gather(cat_factor, "cell", axis=0, tiled=True),
    )
    rank_width = hour_rows.shape[1]
    hours_here = hour_rows.shape[0]
    cats_here = cat_rows.shape[0]
    hour_t = hour_rows.astype(jnp.float32).T
    cat_t = cat_rows.astype(jnp.float32).T
    khatri = (
        (hour_t[:, :, None] * cat_t[:, None, :])
        .reshape(rank_width, hours_here * cats_here)
        .astype(jnp.bfloat16)
    )
    cells_here = demand.shape[2]
    unfolded = demand.reshape(hours_here * cats_here, cells_here)
    hour_gram = lax.psum(
        jnp.dot(hour_rows.T, hour_rows, preferred_element_type=jnp.float32), "hour"
    )
    cat_gram = lax.psum(jnp.dot(cat_rows.T, cat_rows, preferred_element_type=jnp.float32), "cat")
    normal_matrix = hour_gram * cat_gram
    lower_factor = jnp.linalg.cholesky(normal_matrix)
    partial_sums = jnp.dot(khatri, unfolded, preferred_element_type=jnp.float32)
    summed = lax.psum(partial_sums, ("hour", "cat"))
    return jax.scipy.linalg.cho_solve((lower_factor, True), summed)


def solution(mesh):
    in_specs = (P("hour", "cat", "cell"), P(("hour", "cell"), None), P(("cat", "cell"), None))
    out_specs = P(None, "cell")
    return jax.shard_map(shards, mesh=mesh, in_specs=in_specs, out_specs=out_specs, check_vma=False)
```

profile of v0, /device:TPU:1, one launch (start us, length us, event | category | flops | bytes accessed | tf_op | source)
XLA Modules:
  0.0 404.3 jit_solution(17309989984058974652)
XLA Ops:
  6.5 0.0 all-reduce.2.cloned.1.call-start
  6.5 51.7 %all-gather.1 = bf16[16,2,64]{2,1,0:T(2,128)(2,1)S(1)} all-gather(bf16[1,2,64]{2,1,0:T(2,128)(2,1)} %bitcast.33), channel_id=1, replica_groups=mesh['cell'=16,'hour'=8,'cat'=4] {'cell'}, dimensions={0}, use_global_device_ids=true | all-gather | bytes 4352 | tf_op jit(solution)/shard_map/all_gather | solution.py:10
  58.2 0.1 copy.13
  58.3 39.7 %all-gather = bf16[16,4,64]{2,1,0:T(4,128)(2,1)S(1)} all-gather(bf16[1,4,64]{2,1,0:T(4,128)(2,1)} %bitcast.32), channel_id=1, replica_groups=mesh['cell'=16,'hour'=8,'cat'=4] {'cell'}, dimensions={0}, use_global_device_ids=true | all-gather | bytes 8704 | tf_op jit(solution)/shard_map/all_gather | solution.py:9
  98.1 0.1 copy.12
  98.1 0.7 multiply_convert_fusion
  98.8 4.7 %convolution_bitcast_fusion = f32[64,1024]{1,0:T(8,128)} fusion(bf16[64,32,1024]{2,1,0:T(8,128)(2,1)} %param.3, bf16[64,64,32]{2,1,0:T(8,128)(2,1)S(1)} %multiply_convert_fusion), kind=kOutput, calls=%fused_computation.1 | convolution fusion | flops 268435456 | bytes 4718592 | tf_op jit(solution)/shard_map/dot_general | solution.py:30
  103.6 0.0 all-reduce.2.cloned.1.call-update
  103.6 0.2 fusion.7
  103.8 0.2 fusion.8
  104.0 36.8 %psum.21 = f32[64,64]{0,1:T(8,128)S(1)} all-reduce(f32[64,64]{0,1:T(8,128)S(1)} %fusion.7), channel_id=1, replica_groups=mesh['cell'=16,'hour'=8,'cat'=4] {'hour'}, use_global_device_ids=true, to_apply=%region_0.0 | all-reduce | flops 4096 | bytes 32768 | tf_op jit(solution)/shard_map/psum | solution.py:24
  140.8 13.8 %psum.22 = f32[64,64]{0,1:T(8,128)S(1)} all-reduce(f32[64,64]{0,1:T(8,128)S(1)} %fusion.8), channel_id=1, replica_groups=mesh['cell'=16,'hour'=8,'cat'=4] {'cat'}, use_global_device_ids=true, to_apply=%region_1.0 | all-reduce | flops 4096 | bytes 32768 | tf_op jit(solution)/shard_map/psum | solution.py:27
  154.7 0.1 copy.11
  154.8 5.8 %cholesky.16 = f32[64,64]{1,0:T(8,128)S(1)} custom-call(f32[64,64]{1,0:T(8,128)S(1)} %fusion.6), custom_call_target="Cholesky" | custom-call | tf_op jit(solution)/shard_map/jit(cholesky)/cholesky | solution.py:29
  160.7 0.7 compare_reduce_fusion
  161.4 0.6 fusion.1
  162.0 4.9 %custom-call.10 = f32[1,64,64]{1,2,0:T(8,128)S(1)} custom-call(f32[1,64,64]{2,1,0:T(8,128)S(1)} %fusion.1), custom_call_target="InvertDiagBlocksLowerTriangular" | custom-call | tf_op jit(solution)/shard_map/jit(_cho_solve)/triangular_solve | solution.py:32
  166.9 228.1 %all-reduce.2.cloned.1.call-done = f32[64,1024]{1,0:T(8,128)} async-done(((f32[64,1024]{1,0:T(8,128)}), f32[64,1024]{1,0:T(8,128)}) %all-reduce.2.cloned.1.call-update) | async-done | bytes 262160 | tf_op jit(solution)/shard_map/psum | solution.py:31
  395.0 1.4 fusion.4
  396.4 1.1 fusion.2
  (5 shorter events, 0.1 us)
Async XLA Ops:
  6.5 388.5 %all-reduce.2.cloned.1.call-start = ((), (), s32[]{:S(2)}) async-start(), calls=%async_computation | async-start | bytes 524288 | tf_op jit(solution)/shard_map/psum | solution.py:31
Sparse Core Ops, SparseCore 0:
  103.7 291.2 all-reduce.1
where the time goes:
time: 407 us; the launch traced here: 404 us
  waiting for transfers between devices  228 us (56%)
  blocking collectives  142 us (35%)
  between operations  13.5 us (3%)
  other arithmetic  12.8 us (3%)
  matrix products  7.57 us (2%)
    psum x1, waiting for transfers between devices, shards(): summed = lax.psum(partial_sums, ('hour', 'cat'))  228 us
    all_gather x1, blocking collectives, shards(): lax.all_gather(cat_factor, 'cell', axis=0, tiled=True)  51.7 us
    all_gather x1, blocking collectives, shards(): lax.all_gather(hour_factor, 'cell', axis=0, tiled=True)  39.7 us
    psum x1, blocking collectives, shards(): lax.psum(jnp.dot(hour_rows.T, hour_rows, preferred_element_type=jnp.float...  36.8 us
    psum x1, blocking collectives, shards(): lax.psum(jnp.dot(cat_rows.T, cat_rows, preferred_element_type=jnp.float32...  13.8 us
  transfers between devices with their start and end apart: 1, of which 1 were waited for; matrix products, arithmetic and copies ran while one was open for 3% of the time, Pallas kernels for 0%

commit v1 on v0

v1 whole, which is shorter than its diff:
```python
import jax
import jax.numpy as jnp
from jax import lax
from jax.sharding import PartitionSpec as P

REST = ("hour", "cat")


def spread(block, axes, count):
    copies = jnp.broadcast_to(block[None], (count,) + block.shape)
    return lax.all_to_all(copies, axes, 0, 0)


def shards(demand, hour_factor, cat_factor, sizes):
    cell_n, hour_n, cat_n = sizes
    rest_n = hour_n * cat_n
    hour_own, rank = hour_factor.shape
    cat_own = cat_factor.shape[0]
    hours_here, cats_here, cells_here = demand.shape

    own = jnp.concatenate([hour_factor, cat_factor], axis=0)
    own = jnp.pad(own, ((0, 8 - hour_own - cat_own), (0, 128 - rank)))
    rows = spread(own, "cell", cell_n)
    hour_rows = rows[:, :hour_own, :rank].reshape(hours_here, rank)
    cat_rows = rows[:, hour_own : hour_own + cat_own, :rank].reshape(cats_here, rank)

    hour_t = hour_rows.astype(jnp.float32).T
    cat_t = cat_rows.astype(jnp.float32).T
    khatri = (
        (hour_t[:, :, None] * cat_t[:, None, :])
        .reshape(rank, hours_here * cats_here)
        .astype(jnp.bfloat16)
    )
    unfolded = demand.reshape(hours_here * cats_here, cells_here)
    partial = jnp.dot(khatri, unfolded, preferred_element_type=jnp.float32).astype(jnp.bfloat16)
    chunks = partial.reshape(4, 16, 8, 128).transpose(0, 2, 1, 3).reshape(rest_n, 16, 128)

    hour_share = lax.dynamic_slice_in_dim(hour_rows, lax.axis_index("cat") * (hours_here // cat_n), hours_here // cat_n)
    cat_share = lax.dynamic_slice_in_dim(cat_rows, lax.axis_index("hour") * (cats_here // hour_n), cats_here // hour_n)
    cat_share = jnp.pad(cat_share, ((0, 16 - cats_here // hour_n), (0, 0)))
    share = jnp.concatenate([hour_share, cat_share], axis=1)
    message = jnp.concatenate([chunks, jnp.broadcast_to(share[None], (rest_n, 16, 128))], axis=1)
    arrived = lax.all_to_all(message, REST, 0, 0)

    summed = arrived[:, :16].astype(jnp.float32).sum(0).astype(jnp.bfloat16)
    gathered = spread(summed, REST, rest_n)

    factors = arrived[:, 16:].reshape(rest_n * 16, 128)
    grams = jnp.dot(factors.T, factors, preferred_element_type=jnp.float32)
    normal_matrix = grams[:rank, :rank] * grams[rank:, rank:]
    lower_factor = jnp.linalg.cholesky(normal_matrix)

    mttkrp = gathered.reshape(4, 8, 16, 128).transpose(0, 2, 1, 3).reshape(rank, cells_here)
    return jax.scipy.linalg.cho_solve((lower_factor, True), mttkrp.astype(jnp.float32))


def solution(mesh):
    sizes = tuple(mesh.shape[axis] for axis in ("cell", "hour", "cat"))
    in_specs = (P("hour", "cat", "cell"), P(("hour", "cell"), None), P(("cat", "cell"), None))
    out_specs = P(None, "cell")

    def body(demand, hour_factor, cat_factor):
        return shards(demand, hour_factor, cat_factor, sizes)

    return jax.shard_map(body, mesh=mesh, in_specs=in_specs, out_specs=out_specs, check_vma=False)
```

time: 407 us -> 78.7 us (0.19)
  waiting for transfers between devices: 228 us -> 13.7 us
  blocking collectives: 142 us -> 19 us
  starting transfers between devices: 0.01 us -> 22.1 us
  between operations: 13.5 us -> 0.16 us
    psum x1 -> x0, waiting for transfers between devices: 228 us -> none  [shards(): summed = lax.psum(partial_sums, ('hour', 'cat'))]
    all_gather x2 -> x0, blocking collectives: 91.4 us -> none  [the longest x1 51.7 us: shards(): lax.all_gather(cat_factor, 'cell', axis=0, tiled=True)]
    psum x2 -> x0, blocking collectives: 50.7 us -> none  [the longest x1 36.8 us: shards(): lax.psum(jnp.dot(hour_rows.T, hour_rows, preferred_element_type=jnp.float...]
    all_to_all x0 -> x2, starting transfers between devices: none -> 22.1 us  [spread(): return lax.all_to_all(copies, axes, 0, 0)]
    all_to_all x0 -> x1, blocking collectives: none -> 19 us  [shards(): arrived = lax.all_to_all(message, REST, 0, 0)]
    all_to_all x0 -> x2, waiting for transfers between devices: none -> 13.7 us  [spread(): return lax.all_to_all(copies, axes, 0, 0)]
  transfers between devices with their start and end apart: 1 -> 2, of which waited for: 1 -> 1; matrix products, arithmetic and copies ran while one was open for 3% -> 16% of each run, Pallas kernels for 0% -> 0%
where the time goes in v1:
time: 78.7 us; the launch traced here: 78.4 us
  starting transfers between devices  22.1 us (28%)
  blocking collectives  19 us (24%)
  waiting for transfers between devices  13.7 us (17%)
  other arithmetic  13.2 us (17%)
  matrix products  8.59 us (11%)
  local copies, waits for them, and re-layouts  1.61 us (2%)
    all_to_all x2, starting transfers between devices, spread(): return lax.all_to_all(copies, axes, 0, 0)  22.1 us
    all_to_all x1, blocking collectives, shards(): arrived = lax.all_to_all(message, REST, 0, 0)  19 us
    all_to_all x2, waiting for transfers between devices, spread(): return lax.all_to_all(copies, axes, 0, 0)  13.7 us
    dot_general x1, matrix products, shards(): jnp.dot(khatri, unfolded, preferred_element_type=jnp.float32)  6.98 us
    another operation x3, other arithmetic, shards(): lower_factor = jnp.linalg.cholesky(normal_matrix)  6.6 us
    another operation x2, other arithmetic, shards(): jax.scipy.linalg.cho_solve((lower_factor, True), mttkrp.astype(jnp.float32))  5.59 us
  transfers between devices with their start and end apart: 2, of which 1 were waited for; matrix products, arithmetic and copies ran while one was open for 16% of the time, Pallas kernels for 0%

profile of v1, /device:TPU:1, one launch (start us, length us, event | category | flops | bytes accessed | tf_op | source)
XLA Modules:
  0.0 78.4 jit_solution(8898094353962924899)
XLA Ops:
  0.0 0.7 fusion.29
  0.7 0.6 broadcast_in_dim.7
  1.3 18.2 %all-to-all-start = ((bf16[16,8,128]{2,1,0:T(8,128)(2,1)}), bf16[16,8,128]{2,1,0:T(8,128)(2,1)S(1)}, u32[]{:S(2)}, u32[]{:S(2)}) async-start(bf16[16,8,128]{2,1,0:T(8,128)(2,1)} %broadcast_in_dim.7), calls=%async_computation | async-start | bytes 65536 | tf_op jit(solution)/shard_map/all_to_all | solution.py:11
  19.5 13.7 %all-to-all-done = bf16[16,8,128]{2,1,0:T(8,128)(2,1)S(1)} async-done(((bf16[16,8,128]{2,1,0:T(8,128)(2,1)}), bf16[16,8,128]{2,1,0:T(8,128)(2,1)S(1)}, u32[]{:S(2)}, u32[]{:S(2)}) %all-to-all-start) | async-done | bytes 32800 | tf_op jit(solution)/shard_map/all_to_all | solution.py:11
  33.3 0.1 copy.23
  33.4 7.0 %fusion.8 = bf16[8,8,8,128]{3,1,2,0:T(8,128)(2,1)S(1)} fusion(bf16[64,32,1024]{2,1,0:T(8,128)(2,1)} %param.3, f32[64,32]{0,1:T(8,128)S(1)} %convert_bitcast_fusion.1, f32[64,64]{1,0:T(8,128)S(1)} %copy.23), kind=kOutput, calls=%fused_computation.4 | convolution fusion | flops 268763136 | bytes 4349952 | tf_op jit(solution)/shard_map/dot_general | solution.py:35
  40.4 0.1 fusion.23
  40.6 19.0 %all_to_all.15 = bf16[32,32,128]{2,1,0:T(8,128)(2,1)S(1)} all-to-all(bf16[32,32,128]{2,1,0:T(8,128)(2,1)S(1)} %pad_maximum_fusion), channel_id=1, replica_groups=mesh['cell'=16,'hour'=8,'cat'=4] {'hour','cat'}, dimensions={0} | all-to-all | bytes 524288 | tf_op jit(solution)/shard_map/all_to_all | solution.py:43
  59.6 0.2 convolution_bitcast_fusion
  59.8 0.1 slice_multiply_fusion
  59.9 0.1 copy.29
  60.0 0.7 broadcast_in_dim.9
  60.7 3.9 %all-to-all-start.2 = ((bf16[32,16,128]{2,1,0:T(8,128)(2,1)}), bf16[32,16,128]{2,1,0:T(8,128)(2,1)S(1)}, u32[]{:S(2)}, u32[]{:S(2)}) async-start(bf16[32,16,128]{2,1,0:T(8,128)(2,1)} %broadcast_in_dim.9), calls=%async_computation.2 | async-start | bytes 262144 | tf_op jit(solution)/shard_map/all_to_all | solution.py:11
  64.6 0.1 fusion.21
  64.7 5.8 %cholesky.16 = f32[64,64]{1,0:T(8,128)S(1)} custom-call(f32[64,64]{1,0:T(8,128)S(1)} %fusion.21), custom_call_target="Cholesky" | custom-call | tf_op jit(solution)/shard_map/jit(cholesky)/cholesky | solution.py:51
  70.6 0.7 compare_reduce_fusion
  71.3 0.7 fusion.17
  72.0 4.9 %custom-call.10 = f32[1,64,64]{1,2,0:T(8,128)S(1)} custom-call(f32[1,64,64]{2,1,0:T(8,128)S(1)} %fusion.17), custom_call_target="InvertDiagBlocksLowerTriangular" | custom-call | tf_op jit(solution)/shard_map/jit(_cho_solve)/triangular_solve | solution.py:54
  76.9 0.0 all-to-all-done.2
  77.0 0.3 fusion.13
  77.3 1.1 %fusion.18 = f32[64,1024]{1,0:T(8,128)} fusion(f32[64,1024]{1,0:T(8,128)S(1)} %fusion.13, f32[1,64,64]{1,2,0:T(8,128)S(1)} %custom-call.10), kind=kOutput, calls=%fused_computation.19 | convolution fusion | flops 50331648 | bytes 540672 | tf_op jit(solution)/shard_map/jit(_cho_solve)/triangular_solve | solution.py:54
  (14 shorter events, 0.3 us)
Async XLA Ops:
  1.3 31.9 %all-to-all-start = ((bf16[16,8,128]{2,1,0:T(8,128)(2,1)}), bf16[16,8,128]{2,1,0:T(8,128)(2,1)S(1)}, u32[]{:S(2)}, u32[]{:S(2)}) async-start(bf16[16,8,128]{2,1,0:T(8,128)(2,1)} %broadcast_in_dim.7), calls=%async_computation | async-start | bytes 65536 | tf_op jit(solution)/shard_map/all_to_all | solution.py:11
  60.7 16.2 %all-to-all-start.2 = ((bf16[32,16,128]{2,1,0:T(8,128)(2,1)}), bf16[32,16,128]{2,1,0:T(8,128)(2,1)S(1)}, u32[]{:S(2)}, u32[]{:S(2)}) async-start(bf16[32,16,128]{2,1,0:T(8,128)(2,1)} %broadcast_in_dim.9), calls=%async_computation.2 | async-start | bytes 262144 | tf_op jit(solution)/shard_map/all_to_all | solution.py:11

commit v2 on v1

v2 whole, which is shorter than its diff:
```python
import functools

import jax
import jax.numpy as jnp
from jax import lax
from jax.experimental import pallas as pl
from jax.experimental.pallas import tpu as pltpu
from jax.sharding import PartitionSpec as P

REST = ("hour", "cat")
LANES = 128
GROUP = 8
TALL = 16
F32 = jnp.float32
BF16 = jnp.bfloat16


def iota(shape, dim):
    return lax.broadcasted_iota(jnp.int32, shape, dim)


def rows_kernel(hour_ref, cat_ref, out_ref):
    hour_own, rank = hour_ref.shape
    cat_own = cat_ref.shape[0]
    hours = hour_ref[...].astype(F32)
    cats = cat_ref[...].astype(F32)
    cats = jnp.concatenate([cats, jnp.zeros((hour_own - cat_own, rank), F32)], axis=0)
    own = jnp.concatenate([hours, cats], axis=1)
    own = jnp.concatenate([own, jnp.zeros((GROUP - hour_own, LANES), F32)], axis=0)
    out_ref[...] = jnp.broadcast_to(own.astype(BF16)[None], out_ref.shape)


def partial_kernel(rank, hour_own, cat_own, rows_ref, demand_ref, out_ref, groups_ref):
    cell_n = rows_ref.shape[0]
    hours_here, cats_here, cells_here = demand_ref.shape
    depth = hours_here * cats_here
    groups = rows_ref[...].astype(F32)
    groups_ref[...] = groups
    flat = groups.reshape(cell_n * GROUP, LANES)
    turned = flat.T.astype(BF16)
    column = iota((cell_n * GROUP, depth), 1)
    row = iota((cell_n * GROUP, depth), 0)
    hour = column // cats_here
    pick_hour = (row == (hour // hour_own) * GROUP + hour % hour_own).astype(F32).astype(BF16)
    cat = iota((cell_n * GROUP, LANES), 1) % cats_here
    cat_row = iota((cell_n * GROUP, LANES), 0)
    pick_cat = (cat_row == (cat // cat_own) * GROUP + cat % cat_own).astype(F32).astype(BF16)
    hour_cols = jnp.dot(turned[:rank], pick_hour, preferred_element_type=F32)
    cat_cols = jnp.dot(turned[rank:], pick_cat, preferred_element_type=F32)
    cat_cols = jnp.concatenate([cat_cols] * (depth // LANES), axis=1)
    khatri = (hour_cols * cat_cols).astype(BF16)

    width = 256
    across = cells_here // LANES
    for left in range(0, cells_here, width):
        block = demand_ref[:, :, left : left + width].reshape(depth, width)
        sums = jnp.dot(khatri, block, preferred_element_type=F32).astype(BF16)
        for down in range(rank // TALL):
            for over in range(width // LANES):
                out_ref[down * across + left // LANES + over, :TALL, :] = sums[
                    down * TALL : (down + 1) * TALL, over * LANES : (over + 1) * LANES
                ]

    hour_first = lax.axis_index("cat") * (TALL // hour_own)
    cat_groups = cats_here // lax.axis_size("hour") // cat_own
    cat_first = lax.axis_index("hour") * cat_groups
    left_half = iota((hour_own, LANES), 1) < rank
    pieces = []
    for step in range(TALL // hour_own):
        hours = groups_ref[hour_first + step][:hour_own]
        cats = groups_ref[cat_first + step][:hour_own] if step < cat_groups else jnp.zeros_like(hours)
        pieces.append(jnp.where(left_half, hours, cats))
    share = jnp.concatenate(pieces, axis=0).astype(BF16)
    out_ref[:, TALL:, :] = jnp.broadcast_to(share[None], (out_ref.shape[0], TALL, LANES))


def sum_kernel(arrived_ref, out_ref):
    count = arrived_ref.shape[0]
    terms = [arrived_ref[n, :TALL, :].astype(F32) for n in range(count)]
    while len(terms) > 1:
        terms = [terms[n] + terms[n + 1] for n in range(0, len(terms), 2)]
    out_ref[...] = jnp.broadcast_to(terms[0].astype(BF16)[None], out_ref.shape)


def inverse_kernel(rank, arrived_ref, out_ref):
    count = arrived_ref.shape[0]
    rows = arrived_ref[:, TALL:, :].reshape(count * TALL, LANES)
    grams = lax.dot_general(rows, rows, (((0,), (0,)), ((), ())), preferred_element_type=F32)
    normal = grams[:rank] * pltpu.roll(grams[rank:], rank, 1)
    row, lane = iota((rank, LANES), 0), iota((rank, LANES), 1)
    diagonal = jnp.where(row == lane, normal, 0.0)
    by_row = lax.rsqrt(jnp.sum(diagonal, axis=1, keepdims=True))
    mirrored = diagonal + pltpu.roll(diagonal, rank, 1)
    by_lane = lax.rsqrt(jnp.sum(mirrored, axis=0, keepdims=True))
    left_half = lane < rank
    work = jnp.where(left_half, normal * by_row * by_lane, (row + rank == lane).astype(F32))
    blocks = [work[n * 8 : (n + 1) * 8] for n in range(rank // 8)]
    sub = iota((8, LANES), 0)
    for first in range(0, rank, 2):
        home, at = first // 8, first % 8
        columns_a = [jnp.broadcast_to(b[:, first : first + 1], (8, LANES)) for b in blocks]
        columns_b = [jnp.broadcast_to(b[:, first + 1 : first + 2], (8, LANES)) for b in blocks]
        row_a, row_b = blocks[home][at : at + 1], blocks[home][at + 1 : at + 2]
        p_aa, p_ba = columns_a[home][at : at + 1], columns_a[home][at + 1 : at + 2]
        p_ab, p_bb = columns_b[home][at : at + 1], columns_b[home][at + 1 : at + 2]
        scale = 1.0 / (p_aa * p_bb - p_ab * p_ba)
        new_a = (p_bb * row_a - p_ab * row_b) * scale
        new_b = (p_aa * row_b - p_ba * row_a) * scale
        new_a, new_b = jnp.broadcast_to(new_a, (8, LANES)), jnp.broadcast_to(new_b, (8, LANES))
        blocks = [b - (ca * new_a + cb * new_b) for b, ca, cb in zip(blocks, columns_a, columns_b)]
        blocks[home] = jnp.where(sub == at, new_a, jnp.where(sub == at + 1, new_b, blocks[home]))
    inverse = jnp.concatenate(blocks, axis=0) * by_row * by_lane
    inverse = pltpu.roll(inverse, rank, 1)
    high = inverse.astype(BF16)
    rest = inverse - high.astype(F32)
    middle = rest.astype(BF16)
    low = (rest - middle.astype(F32)).astype(BF16)
    out_ref[:rank] = high
    out_ref[rank : 2 * rank] = middle
    out_ref[2 * rank :] = low


def solve_kernel(rank, inverse_ref, sums_ref, out_ref):
    cells_here = out_ref.shape[1]
    across = cells_here // LANES
    lhs = inverse_ref[...][:, :rank]
    for over in range(0, across, 2):
        rhs = jnp.concatenate(
            [
                jnp.concatenate([sums_ref[down * across + over + n] for down in range(rank // TALL)], axis=0)
                for n in range(2)
            ],
            axis=1,
        )
        terms = jnp.dot(lhs, rhs, preferred_element_type=F32)
        out_ref[:, over * LANES : (over + 2) * LANES] = terms[:rank] + (
            terms[rank : 2 * rank] + terms[2 * rank :]
        )


def call(kernel, shape, dtype, operands, flops, moved, scratch=()):
    vmem = pl.BlockSpec(memory_space=pltpu.VMEM)
    return pl.pallas_call(
        kernel,
        out_shape=jax.ShapeDtypeStruct(shape, dtype),
        in_specs=[vmem] * len(operands),
        out_specs=vmem,
        scratch_shapes=list(scratch),
        compiler_params=pltpu.CompilerParams(vmem_limit_bytes=24 * 1024 * 1024),
        cost_estimate=pl.CostEstimate(flops=flops, bytes_accessed=moved, transcendentals=0),
    )(*operands)


def shards(demand, hour_factor, cat_factor, sizes):
    cell_n, hour_n, cat_n = sizes
    rest_n = hour_n * cat_n
    hour_own, rank = hour_factor.shape
    cat_own = cat_factor.shape[0]
    cells_here = demand.shape[2]

    own = call(rows_kernel, (cell_n, GROUP, LANES), BF16, (hour_factor, cat_factor), 1000, 40000)
    rows = lax.all_to_all(own, "cell", 0, 0)
    message = call(
        functools.partial(partial_kernel, rank, hour_own, cat_own),
        (rest_n, 2 * TALL, LANES),
        BF16,
        (rows, demand),
        2 * rank * demand.size,
        2 * demand.size,
        [pltpu.VMEM((cell_n, GROUP, LANES), F32)],
    )
    arrived = lax.all_to_all(message, REST, 0, 0)
    summed = call(sum_kernel, (rest_n, TALL, LANES), BF16, (arrived,), 100000, 400000)
    gathered = lax.all_to_all(summed, REST, 0, 0)
    inverse = call(
        functools.partial(inverse_kernel, rank), (3 * rank, LANES), BF16, (arrived,), 2**24, 10**7
    )
    return call(
        functools.partial(solve_kernel, rank),
        (rank, cells_here),
        F32,
        (inverse, gathered),
        6 * rank * rank * cells_here,
        400000,
    )


def solution(mesh):
    sizes = tuple(mesh.shape[axis] for axis in ("cell", "hour", "cat"))
    in_specs = (P("hour", "cat", "cell"), P(("hour", "cell"), None), P(("cat", "cell"), None))
    out_specs = P(None, "cell")

    def body(demand, hour_factor, cat_factor):
        return shards(demand, hour_factor, cat_factor, sizes)

    return jax.shard_map(body, mesh=mesh, in_specs=in_specs, out_specs=out_specs, check_vma=False)
```

time: 78.7 us -> 69.8 us (0.89)
  blocking collectives: 19 us -> 50.6 us
  starting transfers between devices: 22.1 us -> 3.94 us
  other arithmetic: 13.2 us -> 0 us
  waiting for transfers between devices: 13.7 us -> 4.83 us
  matrix products: 8.59 us -> 0 us
  Pallas kernels: 0 us -> 6.57 us
  local copies, waits for them, and re-layouts: 1.61 us -> 3.52 us
    all_to_all x0 -> x1, blocking collectives: none -> 31.7 us  [shards(): rows = lax.all_to_all(own, 'cell', 0, 0)]
    all_to_all x2 -> x1, starting transfers between devices: 22.1 us -> 3.94 us  [shards(): gathered = lax.all_to_all(summed, REST, 0, 0)]
    another operation x5 -> x0, other arithmetic: 12.2 us -> none  [the longest x3 6.6 us: shards(): lower_factor = jnp.linalg.cholesky(normal_matrix)]
    all_to_all x2 -> x1, waiting for transfers between devices: 13.7 us -> 4.83 us  [shards(): gathered = lax.all_to_all(summed, REST, 0, 0)]
    dot_general x2 -> x0, matrix products: 7.21 us -> none  [the longest x1 6.98 us: shards(): jnp.dot(khatri, unfolded, preferred_element_type=jnp.float32)]
    pallas_call x0 -> x5, Pallas kernels: none -> 6.57 us  [call(): pl.pallas_call(kernel, out_shape=jax.ShapeDtypeStruct(shape, dtype), in_s...]
    unnamed x1 -> x6, local copies, waits for them, and re-layouts: 0.02 us -> 3.52 us
    another operation x2 -> x0, matrix products: 1.38 us -> none  [shards(): jax.scipy.linalg.cho_solve((lower_factor, True), mttkrp.astype(jnp.float32))]
  transfers between devices with their start and end apart: 2 -> 1, of which waited for: 1 -> 1; matrix products, arithmetic and copies ran while one was open for 16% -> 0% of each run, Pallas kernels for 0% -> 5%
where the time goes in v2:
time: 69.8 us; the launch traced here: 69.5 us
  blocking collectives  50.6 us (72%)
  Pallas kernels  6.57 us (9%)
  waiting for transfers between devices  4.83 us (7%)
  starting transfers between devices  3.94 us (6%)
  local copies, waits for them, and re-layouts  3.52 us (5%)
    all_to_all x1, blocking collectives, shards(): rows = lax.all_to_all(own, 'cell', 0, 0)  31.7 us
    all_to_all x1, blocking collectives, shards(): arrived = lax.all_to_all(message, REST, 0, 0)  19 us
    pallas_call x5, Pallas kernels, call(): pl.pallas_call(kernel, out_shape=jax.ShapeDtypeStruct(shape, dtype), in_s...  6.57 us
    all_to_all x1, waiting for transfers between devices, shards(): gathered = lax.all_to_all(summed, REST, 0, 0)  4.83 us
    all_to_all x1, starting transfers between devices, shards(): gathered = lax.all_to_all(summed, REST, 0, 0)  3.94 us
    unnamed x6, local copies, waits for them, and re-layouts  3.52 us
  transfers between devices with their start and end apart: 1, of which 1 were waited for; matrix products, arithmetic and copies ran while one was open for 0% of the time, Pallas kernels for 5%

profile of v2, /device:TPU:1, one launch (start us, length us, event | category | flops | bytes accessed | tf_op | source)
XLA Modules:
  0.0 69.5 jit_solution(14173621120085281218)
XLA Ops:
  0.0 0.0 copy-start.1
  0.0 0.7 copy-done.1
  0.7 0.0 copy-start.2
  0.7 0.7 copy-done.2
  1.3 0.1 shard_map.37
  1.4 31.7 %all_to_all.15.rows_ref = bf16[16,8,128]{2,1,0:T(8,128)(2,1)S(1)} all-to-all(bf16[16,8,128]{2,1,0:T(8,128)(2,1)S(1)} %shard_map.37), channel_id=1, replica_groups=mesh['cell'=16,'hour'=8,'cat'=4] {'cell'}, dimensions={0} | all-to-all | bytes 65536 | tf_op jit(solution)/shard_map/all_to_all | solution.py:162
  33.1 0.0 copy-start
  33.1 2.2 %copy-done = bf16[64,32,1024]{2,1,0:T(8,128)(2,1)S(1)} copy-done((bf16[64,32,1024]{2,1,0:T(8,128)(2,1)S(1)}, bf16[64,32,1024]{2,1,0:T(8,128)(2,1)}, u32[]{:S(2)}) %copy-start) | copy-done | bytes 4194328
  35.3 1.1 %shard_map.38 = bf16[32,32,128]{2,1,0:T(8,128)(2,1)S(1)} custom-call(bf16[16,8,128]{2,1,0:T(8,128)(2,1)S(1)} %all_to_all.15.rows_ref, bf16[64,32,1024]{2,1,0:T(8,128)(2,1)S(1)} %copy-done), custom_call_target="tpu_custom_call" | custom-call | flops 268435456 | bytes 4194304 | tf_op jit(solution)/shard_map/pallas_call | solution.py:143
  36.4 19.0 %all_to_all.16.arrived_ref = bf16[32,32,128]{2,1,0:T(8,128)(2,1)S(1)} all-to-all(bf16[32,32,128]{2,1,0:T(8,128)(2,1)S(1)} %shard_map.38), channel_id=1, replica_groups=mesh['cell'=16,'hour'=8,'cat'=4] {'hour','cat'}, dimensions={0} | all-to-all | bytes 524288 | tf_op jit(solution)/shard_map/all_to_all | solution.py:172
  55.4 0.7 shard_map.40
  56.0 3.9 %all-to-all-start.2 = ((bf16[32,16,128]{2,1,0:T(8,128)(2,1)}), bf16[32,16,128]{2,1,0:T(8,128)(2,1)S(1)}, u32[]{:S(2)}, u32[]{:S(2)}) async-start(bf16[32,16,128]{2,1,0:T(8,128)(2,1)} %shard_map.40), calls=%async_computation.2 | async-start | bytes 262144 | tf_op jit(solution)/shard_map/all_to_all | solution.py:174
  60.0 3.7 %shard_map.39.inverse_ref = bf16[192,128]{1,0:T(8,128)(2,1)S(1)} custom-call(bf16[32,32,128]{2,1,0:T(8,128)(2,1)S(1)} %all_to_all.16.arrived_ref), custom_call_target="tpu_custom_call" | custom-call | flops 16777216 | bytes 10000000 | tf_op jit(solution)/shard_map/pallas_call | solution.py:143
  63.8 4.8 %all-to-all-done.2.sums_ref = bf16[32,16,128]{2,1,0:T(8,128)(2,1)S(1)} async-done(((bf16[32,16,128]{2,1,0:T(8,128)(2,1)}), bf16[32,16,128]{2,1,0:T(8,128)(2,1)S(1)}, u32[]{:S(2)}, u32[]{:S(2)}) %all-to-all-start.2) | async-done | bytes 131104 | tf_op jit(solution)/shard_map/all_to_all | solution.py:174
  68.6 0.9 %shard_map.41 = f32[64,1024]{1,0:T(8,128)} custom-call(bf16[192,128]{1,0:T(8,128)(2,1)S(1)} %shard_map.39.inverse_ref, bf16[32,16,128]{2,1,0:T(8,128)(2,1)S(1)} %all-to-all-done.2.sums_ref), custom_call_target="tpu_custom_call" | custom-call | flops 25165824 | bytes 400000 | tf_op jit(solution)/shard_map/pallas_call | solution.py:143
Async XLA Ops:
  0.0 0.7 copy-start.1
  0.7 0.7 copy-start.2
  33.1 2.2 %copy-start = (bf16[64,32,1024]{2,1,0:T(8,128)(2,1)S(1)}, bf16[64,32,1024]{2,1,0:T(8,128)(2,1)}, u32[]{:S(2)}) copy-start(bf16[64,32,1024]{2,1,0:T(8,128)(2,1)} %demand_ref.1) | copy-start | bytes 12582916
  56.0 12.5 %all-to-all-start.2 = ((bf16[32,16,128]{2,1,0:T(8,128)(2,1)}), bf16[32,16,128]{2,1,0:T(8,128)(2,1)S(1)}, u32[]{:S(2)}, u32[]{:S(2)}) async-start(bf16[32,16,128]{2,1,0:T(8,128)(2,1)} %shard_map.40), calls=%async_computation.2 | async-start | bytes 262144 | tf_op jit(solution)/shard_map/all_to_all | solution.py:174

commit v3 on v2

--- a/solution.py
+++ b/solution.py
@@ -13,24 +13,24 @@
 TALL = 16
 F32 = jnp.float32
 BF16 = jnp.bfloat16
+STRIP = 8
 
 
 def iota(shape, dim):
     return lax.broadcasted_iota(jnp.int32, shape, dim)
 
 
-def rows_kernel(hour_ref, cat_ref, out_ref):
-    hour_own, rank = hour_ref.shape
-    cat_own = cat_ref.shape[0]
-    hours = hour_ref[...].astype(F32)
-    cats = cat_ref[...].astype(F32)
-    cats = jnp.concatenate([cats, jnp.zeros((hour_own - cat_own, rank), F32)], axis=0)
-    own = jnp.concatenate([hours, cats], axis=1)
-    own = jnp.concatenate([own, jnp.zeros((GROUP - hour_own, LANES), F32)], axis=0)
-    out_ref[...] = jnp.broadcast_to(own.astype(BF16)[None], out_ref.shape)
-
-
-def partial_kernel(rank, hour_own, cat_own, rows_ref, demand_ref, out_ref, groups_ref):
+def rows_kernel(own_ref, out_ref):
+    out_ref[...] = jnp.broadcast_to(own_ref[...][None], out_ref.shape)
+
+
+def partial_kernel(rank, hour_own, cat_own, rows_ref, demand_in, out_ref, groups_ref, demand_ref, sems):
+    width = 256
+    copies = []
+    for n in range(demand_in.shape[0] // STRIP):
+        part = pl.ds(n * STRIP, STRIP)
+        copies.append(pltpu.make_async_copy(demand_in.at[part], demand_ref.at[part], sems.at[n]))
+        copies[-1].start()
     cell_n = rows_ref.shape[0]
     hours_here, cats_here, cells_here = demand_ref.shape
     depth = hours_here * cats_here
@@ -50,17 +50,6 @@
     cat_cols = jnp.concatenate([cat_cols] * (depth // LANES), axis=1)
     khatri = (hour_cols * cat_cols).astype(BF16)
 
-    width = 256
-    across = cells_here // LANES
-    for left in range(0, cells_here, width):
-        block = demand_ref[:, :, left : left + width].reshape(depth, width)
-        sums = jnp.dot(khatri, block, preferred_element_type=F32).astype(BF16)
-        for down in range(rank // TALL):
-            for over in range(width // LANES):
-                out_ref[down * across + left // LANES + over, :TALL, :] = sums[
-                    down * TALL : (down + 1) * TALL, over * LANES : (over + 1) * LANES
-                ]
-
     hour_first = lax.axis_index("cat") * (TALL // hour_own)
     cat_groups = cats_here // lax.axis_size("hour") // cat_own
     cat_first = lax.axis_index("hour") * cat_groups
@@ -72,6 +61,23 @@
         pieces.append(jnp.where(left_half, hours, cats))
     share = jnp.concatenate(pieces, axis=0).astype(BF16)
     out_ref[:, TALL:, :] = jnp.broadcast_to(share[None], (out_ref.shape[0], TALL, LANES))
+
+    across = cells_here // LANES
+    chunk = STRIP * cats_here
+    totals = [0.0] * (cells_here // width)
+    for n, copy in enumerate(copies):
+        copy.wait()
+        columns = khatri[:, n * chunk : (n + 1) * chunk]
+        for strip in range(len(totals)):
+            block = demand_ref[n * STRIP : (n + 1) * STRIP, :, strip * width : (strip + 1) * width]
+            totals[strip] += jnp.dot(columns, block.reshape(chunk, width), preferred_element_type=F32)
+    for strip, total in enumerate(totals):
+        left, sums = strip * width, total.astype(BF16)
+        for down in range(rank // TALL):
+            for over in range(width // LANES):
+                out_ref[down * across + left // LANES + over, :TALL, :] = sums[
+                    down * TALL : (down + 1) * TALL, over * LANES : (over + 1) * LANES
+                ]
 
 
 def sum_kernel(arrived_ref, out_ref):
@@ -120,7 +126,8 @@
     out_ref[2 * rank :] = low
 
 
-def solve_kernel(rank, inverse_ref, sums_ref, out_ref):
+def solve_kernel(rank, inverse_ref, sums_ref, out_hbm, out_ref, sems):
+    copies = []
     cells_here = out_ref.shape[1]
     across = cells_here // LANES
     lhs = inverse_ref[...][:, :rank]
@@ -136,17 +143,22 @@
         out_ref[:, over * LANES : (over + 2) * LANES] = terms[:rank] + (
             terms[rank : 2 * rank] + terms[2 * rank :]
         )
-
-
-def call(kernel, shape, dtype, operands, flops, moved, scratch=()):
-    vmem = pl.BlockSpec(memory_space=pltpu.VMEM)
+        part = pl.ds(over * LANES, 2 * LANES)
+        copies.append(pltpu.make_async_copy(out_ref.at[:, part], out_hbm.at[:, part], sems.at[over // 2]))
+        copies[-1].start()
+    for copy in copies:
+        copy.wait()
+
+
+def call(kernel, shape, dtype, operands, flops, moved, scratch=(), left=(), leave_out=False, mib=24):
+    vmem, anywhere = pl.BlockSpec(memory_space=pltpu.VMEM), pl.BlockSpec(memory_space=pltpu.HBM)
     return pl.pallas_call(
         kernel,
         out_shape=jax.ShapeDtypeStruct(shape, dtype),
-        in_specs=[vmem] * len(operands),
-        out_specs=vmem,
+        in_specs=[anywhere if n in left else vmem for n in range(len(operands))],
+        out_specs=anywhere if leave_out else vmem,
         scratch_shapes=list(scratch),
-        compiler_params=pltpu.CompilerParams(vmem_limit_bytes=24 * 1024 * 1024),
+        compiler_params=pltpu.CompilerParams(vmem_limit_bytes=mib * 1024 * 1024),
         cost_estimate=pl.CostEstimate(flops=flops, bytes_accessed=moved, transcendentals=0),
     )(*operands)
 
@@ -158,7 +170,14 @@
     cat_own = cat_factor.shape[0]
     cells_here = demand.shape[2]
 
-    own = call(rows_kernel, (cell_n, GROUP, LANES), BF16, (hour_factor, cat_factor), 1000, 40000)
+    own = jnp.concatenate(
+        [
+            jnp.pad(hour_factor, ((0, GROUP - hour_own), (0, 0))),
+            jnp.pad(cat_factor, ((0, GROUP - cat_own), (0, 0))),
+        ],
+        axis=1,
+    )
+    own = call(rows_kernel, (cell_n, GROUP, LANES), BF16, (own,), 1000, 40000)
     rows = lax.all_to_all(own, "cell", 0, 0)
     message = call(
         functools.partial(partial_kernel, rank, hour_own, cat_own),
@@ -167,7 +186,13 @@
         (rows, demand),
         2 * rank * demand.size,
         2 * demand.size,
-        [pltpu.VMEM((cell_n, GROUP, LANES), F32)],
+        [
+            pltpu.VMEM((cell_n, GROUP, LANES), F32),
+            pltpu.VMEM(demand.shape, BF16),
+            pltpu.SemaphoreType.DMA((demand.shape[0] // STRIP,)),
+        ],
+        (1,),
+        mib=50,
     )
     arrived = lax.all_to_all(message, REST, 0, 0)
     summed = call(sum_kernel, (rest_n, TALL, LANES), BF16, (arrived,), 100000, 400000)
@@ -182,6 +207,9 @@
         (inverse, gathered),
         6 * rank * rank * cells_here,
         400000,
+        [pltpu.VMEM((rank, cells_here), F32), pltpu.SemaphoreType.DMA((cells_here // LANES // 2,))],
+        (),
+        True,
     )
 
 

time: 69.8 us -> 68.3 us (0.979)
  local copies, waits for them, and re-layouts: 3.52 us -> 0 us
  Pallas kernels: 6.57 us -> 7.79 us
  other arithmetic: 0 us -> 0.77 us
    unnamed x6 -> x0, local copies, waits for them, and re-layouts: 3.52 us -> none
    pallas_call x5, Pallas kernels: 6.57 us -> 7.79 us  [call(): pl.pallas_call(kernel, out_shape=jax.ShapeDtypeStruct(shape, dtype), in_s...]
    concatenate x0 -> x1, other arithmetic: none -> 0.77 us  [shards(): jnp.concatenate([jnp.pad(hour_factor, ((0, GROUP - hour_own), (0, 0))), j...]
  transfers between devices with their start and end apart: 1 -> 1, of which waited for: 1 -> 1; matrix products, arithmetic and copies ran while one was open for 0% -> 0% of each run, Pallas kernels for 5% -> 6%
where the time goes in v3:
time: 68.3 us; the launch traced here: 68 us
  blocking collectives  50.6 us (74%)
  Pallas kernels  7.79 us (11%)
  waiting for transfers between devices  4.83 us (7%)
  starting transfers between devices  3.94 us (6%)
  other arithmetic  0.77 us (1%)
    all_to_all x1, blocking collectives, shards(): rows = lax.all_to_all(own, 'cell', 0, 0)  31.7 us
    all_to_all x1, blocking collectives, shards(): arrived = lax.all_to_all(message, REST, 0, 0)  19 us
    pallas_call x5, Pallas kernels, call(): pl.pallas_call(kernel, out_shape=jax.ShapeDtypeStruct(shape, dtype), in_s...  7.79 us
    all_to_all x1, waiting for transfers between devices, shards(): gathered = lax.all_to_all(summed, REST, 0, 0)  4.83 us
    all_to_all x1, starting transfers between devices, shards(): gathered = lax.all_to_all(summed, REST, 0, 0)  3.94 us
  transfers between devices with their start and end apart: 1, of which 1 were waited for; matrix products, arithmetic and copies ran while one was open for 0% of the time, Pallas kernels for 6%

profile of v3, /device:TPU:1, one launch (start us, length us, event | category | flops | bytes accessed | tf_op | source)
XLA Modules:
  0.0 68.0 jit_solution(3773884305766875332)
XLA Ops:
  0.0 0.8 %fusion.2.own_ref = bf16[8,128]{1,0:T(8,128)(2,1)S(1)} fusion(bf16[2,64]{1,0:T(2,128)(2,1)} %param.5, bf16[4,64]{1,0:T(4,128)(2,1)} %param.4), kind=kLoop, calls=%fused_computation.4 | loop fusion | flops 8192 | bytes 2816 | tf_op jit(solution)/shard_map/concatenate | solution.py:173
  0.8 31.7 %all_to_all.15.rows_ref = bf16[16,8,128]{2,1,0:T(8,128)(2,1)S(1)} all-to-all(bf16[16,8,128]{2,1,0:T(8,128)(2,1)S(1)} %shard_map.37), channel_id=1, replica_groups=mesh['cell'=16,'hour'=8,'cat'=4] {'cell'}, dimensions={0} | all-to-all | bytes 65536 | tf_op jit(solution)/shard_map/all_to_all | solution.py:181
  32.5 2.4 %shard_map.38 = bf16[32,32,128]{2,1,0:T(8,128)(2,1)S(1)} custom-call(bf16[16,8,128]{2,1,0:T(8,128)(2,1)S(1)} %all_to_all.15.rows_ref, bf16[64,32,1024]{2,1,0:T(8,128)(2,1)} %demand_in.1), custom_call_target="tpu_custom_call" | custom-call | flops 268435456 | bytes 4194304 | tf_op jit(solution)/shard_map/pallas_call | solution.py:155
  34.9 19.0 %all_to_all.16.arrived_ref = bf16[32,32,128]{2,1,0:T(8,128)(2,1)S(1)} all-to-all(bf16[32,32,128]{2,1,0:T(8,128)(2,1)S(1)} %shard_map.38), channel_id=1, replica_groups=mesh['cell'=16,'hour'=8,'cat'=4] {'hour','cat'}, dimensions={0} | all-to-all | bytes 524288 | tf_op jit(solution)/shard_map/all_to_all | solution.py:197
  53.9 0.7 %shard_map.40 = bf16[32,16,128]{2,1,0:T(8,128)(2,1)} custom-call(bf16[32,32,128]{2,1,0:T(8,128)(2,1)S(1)} %all_to_all.16.arrived_ref), custom_call_target="tpu_custom_call" | custom-call | flops 100000 | bytes 400000 | tf_op jit(solution)/shard_map/pallas_call | solution.py:155
  54.6 3.9 %all-to-all-start.2 = ((bf16[32,16,128]{2,1,0:T(8,128)(2,1)}), bf16[32,16,128]{2,1,0:T(8,128)(2,1)S(1)}, u32[]{:S(2)}, u32[]{:S(2)}) async-start(bf16[32,16,128]{2,1,0:T(8,128)(2,1)} %shard_map.40), calls=%async_computation.2 | async-start | bytes 262144 | tf_op jit(solution)/shard_map/all_to_all | solution.py:199
  58.5 3.7 %shard_map.39.inverse_ref = bf16[192,128]{1,0:T(8,128)(2,1)S(1)} custom-call(bf16[32,32,128]{2,1,0:T(8,128)(2,1)S(1)} %all_to_all.16.arrived_ref), custom_call_target="tpu_custom_call" | custom-call | flops 16777216 | bytes 10000000 | tf_op jit(solution)/shard_map/pallas_call | solution.py:155
  62.3 4.8 %all-to-all-done.2.sums_ref = bf16[32,16,128]{2,1,0:T(8,128)(2,1)S(1)} async-done(((bf16[32,16,128]{2,1,0:T(8,128)(2,1)}), bf16[32,16,128]{2,1,0:T(8,128)(2,1)S(1)}, u32[]{:S(2)}, u32[]{:S(2)}) %all-to-all-start.2) | async-done | bytes 131104 | tf_op jit(solution)/shard_map/all_to_all | solution.py:199
  67.1 0.9 %shard_map.41 = f32[64,1024]{1,0:T(8,128)} custom-call(bf16[192,128]{1,0:T(8,128)(2,1)S(1)} %shard_map.39.inverse_ref, bf16[32,16,128]{2,1,0:T(8,128)(2,1)S(1)} %all-to-all-done.2.sums_ref), custom_call_target="tpu_custom_call" | custom-call | flops 25165824 | bytes 400000 | tf_op jit(solution)/shard_map/pallas_call | solution.py:155
  (1 shorter events, 0.0 us)
Async XLA Ops:
  54.6 12.5 %all-to-all-start.2 = ((bf16[32,16,128]{2,1,0:T(8,128)(2,1)}), bf16[32,16,128]{2,1,0:T(8,128)(2,1)S(1)}, u32[]{:S(2)}, u32[]{:S(2)}) async-start(bf16[32,16,128]{2,1,0:T(8,128)(2,1)} %shard_map.40), calls=%async_computation.2 | async-start | bytes 262144 | tf_op jit(solution)/shard_map/all_to_all | solution.py:199

commit v4 on v3

--- a/solution.py
+++ b/solution.py
@@ -13,11 +13,18 @@
 TALL = 16
 F32 = jnp.float32
 BF16 = jnp.bfloat16
+CELL_FIRST = 10
+REST_FIRST = 22
 STRIP = 8
 
 
 def iota(shape, dim):
     return lax.broadcasted_iota(jnp.int32, shape, dim)
+
+
+def exchange(blocks, axes, first):
+    order = [n ^ first for n in range(blocks.shape[0])]
+    return lax.all_to_all(blocks, axes, 0, 0, axis_index_groups=[order])
 
 
 def rows_kernel(own_ref, out_ref):
@@ -41,10 +48,10 @@
     column = iota((cell_n * GROUP, depth), 1)
     row = iota((cell_n * GROUP, depth), 0)
     hour = column // cats_here
-    pick_hour = (row == (hour // hour_own) * GROUP + hour % hour_own).astype(F32).astype(BF16)
+    pick_hour = (row == ((hour // hour_own) ^ CELL_FIRST) * GROUP + hour % hour_own).astype(F32).astype(BF16)
     cat = iota((cell_n * GROUP, LANES), 1) % cats_here
     cat_row = iota((cell_n * GROUP, LANES), 0)
-    pick_cat = (cat_row == (cat // cat_own) * GROUP + cat % cat_own).astype(F32).astype(BF16)
+    pick_cat = (cat_row == ((cat // cat_own) ^ CELL_FIRST) * GROUP + cat % cat_own).astype(F32).astype(BF16)
     hour_cols = jnp.dot(turned[:rank], pick_hour, preferred_element_type=F32)
     cat_cols = jnp.dot(turned[rank:], pick_cat, preferred_element_type=F32)
     cat_cols = jnp.concatenate([cat_cols] * (depth // LANES), axis=1)
@@ -178,7 +185,7 @@
         axis=1,
     )
     own = call(rows_kernel, (cell_n, GROUP, LANES), BF16, (own,), 1000, 40000)
-    rows = lax.all_to_all(own, "cell", 0, 0)
+    rows = exchange(own, "cell", CELL_FIRST)
     message = call(
         functools.partial(partial_kernel, rank, hour_own, cat_own),
         (rest_n, 2 * TALL, LANES),
@@ -194,9 +201,9 @@
         (1,),
         mib=50,
     )
-    arrived = lax.all_to_all(message, REST, 0, 0)
+    arrived = exchange(message, REST, REST_FIRST)
     summed = call(sum_kernel, (rest_n, TALL, LANES), BF16, (arrived,), 100000, 400000)
-    gathered = lax.all_to_all(summed, REST, 0, 0)
+    gathered = exchange(summed, REST, REST_FIRST)
     inverse = call(
         functools.partial(inverse_kernel, rank), (3 * rank, LANES), BF16, (arrived,), 2**24, 10**7
     )

time: 68.3 us -> 54.5 us (0.80)
  blocking collectives: 50.6 us -> 38 us
  waiting for transfers between devices: 4.83 us -> 0.51 us
  starting transfers between devices: 3.94 us -> 7.18 us
    all_to_all x2, blocking collectives: 50.6 us -> 38 us  [exchange(): return lax.all_to_all(blocks, axes, 0, 0, axis_index_groups=[order])]
    all_to_all x1, waiting for transfers between devices: 4.83 us -> 0.51 us  [exchange(): return lax.all_to_all(blocks, axes, 0, 0, axis_index_groups=[order])]
    all_to_all x1, starting transfers between devices: 3.94 us -> 7.18 us  [exchange(): return lax.all_to_all(blocks, axes, 0, 0, axis_index_groups=[order])]
  transfers between devices with their start and end apart: 1 -> 1, of which waited for: 1 -> 1; matrix products, arithmetic and copies ran while one was open for 0% -> 0% of each run, Pallas kernels for 6% -> 7%
where the time goes in v4:
time: 54.5 us; the launch traced here: 54.3 us
  blocking collectives  38 us (70%)
  Pallas kernels  7.8 us (14%)
  starting transfers between devices  7.18 us (13%)
  other arithmetic  0.77 us (1%)
    all_to_all x2, blocking collectives, exchange(): return lax.all_to_all(blocks, axes, 0, 0, axis_index_groups=[order])  38 us
    pallas_call x5, Pallas kernels, call(): pl.pallas_call(kernel, out_shape=jax.ShapeDtypeStruct(shape, dtype), in_s...  7.8 us
    all_to_all x1, starting transfers between devices, exchange(): return lax.all_to_all(blocks, axes, 0, 0, axis_index_groups=[order])  7.18 us
  transfers between devices with their start and end apart: 1, of which 1 were waited for; matrix products, arithmetic and copies ran while one was open for 0% of the time, Pallas kernels for 7%

profile of v4, /device:TPU:1, one launch (start us, length us, event | category | flops | bytes accessed | tf_op | source)
XLA Modules:
  0.0 54.3 jit_solution(504499757640894532)
XLA Ops:
  0.0 0.8 %fusion.2.own_ref = bf16[8,128]{1,0:T(8,128)(2,1)S(1)} fusion(bf16[2,64]{1,0:T(2,128)(2,1)} %param.5, bf16[4,64]{1,0:T(4,128)(2,1)} %param.4), kind=kLoop, calls=%fused_computation.4 | loop fusion | flops 8192 | bytes 2816 | tf_op jit(solution)/shard_map/concatenate | solution.py:180
  0.8 22.6 %all_to_all.15.rows_ref = bf16[16,8,128]{2,1,0:T(8,128)(2,1)S(1)} all-to-all(bf16[16,8,128]{2,1,0:T(8,128)(2,1)S(1)} %shard_map.37), channel_id=1, replica_groups={{320,352,256,288,448,480,384,416,64,96,0,32,192,224,128,160},{321,353,2..., dimensions={0} | all-to-all | bytes 65536 | tf_op jit(solution)/shard_map/all_to_all | solution.py:27
  23.4 2.4 %shard_map.38 = bf16[32,32,128]{2,1,0:T(8,128)(2,1)S(1)} custom-call(bf16[16,8,128]{2,1,0:T(8,128)(2,1)S(1)} %all_to_all.15.rows_ref, bf16[64,32,1024]{2,1,0:T(8,128)(2,1)} %demand_in.1), custom_call_target="tpu_custom_call" | custom-call | flops 268435456 | bytes 4194304 | tf_op jit(solution)/shard_map/pallas_call | solution.py:162
  25.9 15.3 %all_to_all.16.arrived_ref = bf16[32,32,128]{2,1,0:T(8,128)(2,1)S(1)} all-to-all(bf16[32,32,128]{2,1,0:T(8,128)(2,1)S(1)} %shard_map.38), channel_id=1, replica_groups={{22,23,20,21,18,19,16,17,30,31,28,29,26,27,24,25,6,7,4,5,2,3,0,1,14,15,..., dimensions={0} | all-to-all | bytes 524288 | tf_op jit(solution)/shard_map/all_to_all | solution.py:27
  41.2 0.7 %shard_map.40 = bf16[32,16,128]{2,1,0:T(8,128)(2,1)} custom-call(bf16[32,32,128]{2,1,0:T(8,128)(2,1)S(1)} %all_to_all.16.arrived_ref), custom_call_target="tpu_custom_call" | custom-call | flops 100000 | bytes 400000 | tf_op jit(solution)/shard_map/pallas_call | solution.py:162
  41.9 7.2 %all-to-all-start.2 = ((bf16[32,16,128]{2,1,0:T(8,128)(2,1)}), bf16[32,16,128]{2,1,0:T(8,128)(2,1)S(1)}, u32[]{:S(2)}, u32[]{:S(2)}) async-start(bf16[32,16,128]{2,1,0:T(8,128)(2,1)} %shard_map.40), calls=%async_computation.2 | async-start | bytes 262144 | tf_op jit(solution)/shard_map/all_to_all | solution.py:27
  49.1 3.7 %shard_map.39.inverse_ref = bf16[192,128]{1,0:T(8,128)(2,1)S(1)} custom-call(bf16[32,32,128]{2,1,0:T(8,128)(2,1)S(1)} %all_to_all.16.arrived_ref), custom_call_target="tpu_custom_call" | custom-call | flops 16777216 | bytes 10000000 | tf_op jit(solution)/shard_map/pallas_call | solution.py:162
  52.8 0.5 all-to-all-done.2.sums_ref
  53.3 0.9 %shard_map.41 = f32[64,1024]{1,0:T(8,128)} custom-call(bf16[192,128]{1,0:T(8,128)(2,1)S(1)} %shard_map.39.inverse_ref, bf16[32,16,128]{2,1,0:T(8,128)(2,1)S(1)} %all-to-all-done.2.sums_ref), custom_call_target="tpu_custom_call" | custom-call | flops 25165824 | bytes 400000 | tf_op jit(solution)/shard_map/pallas_call | solution.py:162
  (1 shorter events, 0.0 us)
Async XLA Ops:
  41.9 11.5 %all-to-all-start.2 = ((bf16[32,16,128]{2,1,0:T(8,128)(2,1)}), bf16[32,16,128]{2,1,0:T(8,128)(2,1)S(1)}, u32[]{:S(2)}, u32[]{:S(2)}) async-start(bf16[32,16,128]{2,1,0:T(8,128)(2,1)} %shard_map.40), calls=%async_computation.2 | async-start | bytes 262144 | tf_op jit(solution)/shard_map/all_to_all | solution.py:27

commit v5 on v4

--- a/solution.py
+++ b/solution.py
@@ -11,6 +11,8 @@
 LANES = 128
 GROUP = 8
 TALL = 16
+SUMS = 8
+HOURS = 4
 F32 = jnp.float32
 BF16 = jnp.bfloat16
 CELL_FIRST = 10
@@ -57,17 +59,19 @@
     cat_cols = jnp.concatenate([cat_cols] * (depth // LANES), axis=1)
     khatri = (hour_cols * cat_cols).astype(BF16)
 
+    left_half = iota((GROUP, LANES), 1) < rank
     hour_first = lax.axis_index("cat") * (TALL // hour_own)
-    cat_groups = cats_here // lax.axis_size("hour") // cat_own
-    cat_first = lax.axis_index("hour") * cat_groups
-    left_half = iota((hour_own, LANES), 1) < rank
-    pieces = []
-    for step in range(TALL // hour_own):
-        hours = groups_ref[hour_first + step][:hour_own]
-        cats = groups_ref[cat_first + step][:hour_own] if step < cat_groups else jnp.zeros_like(hours)
-        pieces.append(jnp.where(left_half, hours, cats))
-    share = jnp.concatenate(pieces, axis=0).astype(BF16)
-    out_ref[:, TALL:, :] = jnp.broadcast_to(share[None], (out_ref.shape[0], TALL, LANES))
+    hours = [groups_ref[hour_first + step][:hour_own] for step in range(TALL // hour_own)]
+    over = jnp.concatenate(hours[:2], axis=0)
+    under = jnp.concatenate(hours[2:], axis=0)
+    share = jnp.where(left_half, over, pltpu.roll(under, rank, 1)).astype(BF16)
+    out_ref[:, SUMS : SUMS + HOURS] = jnp.broadcast_to(
+        share.reshape(1, HOURS, 2, LANES), (out_ref.shape[0], HOURS, 2, LANES)
+    )
+    cat_first = lax.axis_index("hour") * 2
+    over, under = groups_ref[cat_first], groups_ref[cat_first + 1]
+    share = jnp.where(left_half, pltpu.roll(over, rank, 1), under)[:cat_own].astype(BF16)
+    out_ref[:, SUMS + HOURS] = jnp.broadcast_to(share[None], (out_ref.shape[0], 2, LANES))
 
     across = cells_here // LANES
     chunk = STRIP * cats_here
@@ -82,24 +86,26 @@
         left, sums = strip * width, total.astype(BF16)
         for down in range(rank // TALL):
             for over in range(width // LANES):
-                out_ref[down * across + left // LANES + over, :TALL, :] = sums[
-                    down * TALL : (down + 1) * TALL, over * LANES : (over + 1) * LANES
-                ]
+                piece = sums[down * TALL : (down + 1) * TALL, over * LANES : (over + 1) * LANES]
+                out_ref[down * across + left // LANES + over, :SUMS] = piece.reshape(SUMS, 2, LANES)
 
 
 def sum_kernel(arrived_ref, out_ref):
     count = arrived_ref.shape[0]
-    terms = [arrived_ref[n, :TALL, :].astype(F32) for n in range(count)]
+    terms = [arrived_ref[n, :SUMS].astype(F32) for n in range(count)]
     while len(terms) > 1:
         terms = [terms[n] + terms[n + 1] for n in range(0, len(terms), 2)]
-    out_ref[...] = jnp.broadcast_to(terms[0].astype(BF16)[None], out_ref.shape)
+    out_ref[...] = jnp.broadcast_to(terms[0].reshape(TALL, LANES).astype(BF16)[None], out_ref.shape)
+
+
+def gram(pairs, rank):
+    rows = pairs.astype(F32).reshape(-1, LANES).astype(BF16)
+    both = lax.dot_general(rows, rows, (((0,), (0,)), ((), ())), preferred_element_type=F32)
+    return both[:rank] + pltpu.roll(both[rank:], rank, 1)
 
 
 def inverse_kernel(rank, arrived_ref, out_ref):
-    count = arrived_ref.shape[0]
-    rows = arrived_ref[:, TALL:, :].reshape(count * TALL, LANES)
-    grams = lax.dot_general(rows, rows, (((0,), (0,)), ((), ())), preferred_element_type=F32)
-    normal = grams[:rank] * pltpu.roll(grams[rank:], rank, 1)
+    normal = gram(arrived_ref[:, SUMS : SUMS + HOURS], rank) * gram(arrived_ref[:, SUMS + HOURS], rank)
     row, lane = iota((rank, LANES), 0), iota((rank, LANES), 1)
     diagonal = jnp.where(row == lane, normal, 0.0)
     by_row = lax.rsqrt(jnp.sum(diagonal, axis=1, keepdims=True))
@@ -188,7 +194,7 @@
     rows = exchange(own, "cell", CELL_FIRST)
     message = call(
         functools.partial(partial_kernel, rank, hour_own, cat_own),
-        (rest_n, 2 * TALL, LANES),
+        (rest_n, SUMS + HOURS + 1, 2, LANES),
         BF16,
         (rows, demand),
         2 * rank * demand.size,

time: 54.5 us -> 53.7 us (0.985)
  blocking collectives: 38 us -> 37 us
    all_to_all x2, blocking collectives: 38 us -> 37 us  [exchange(): return lax.all_to_all(blocks, axes, 0, 0, axis_index_groups=[order])]
where the time goes in v5:
time: 53.7 us; the launch traced here: 53.4 us
  blocking collectives  37 us (69%)
  Pallas kernels  8.1 us (15%)
  starting transfers between devices  7.09 us (13%)
  other arithmetic  0.77 us (1%)
    all_to_all x2, blocking collectives, exchange(): return lax.all_to_all(blocks, axes, 0, 0, axis_index_groups=[order])  37 us
    pallas_call x5, Pallas kernels, call(): pl.pallas_call(kernel, out_shape=jax.ShapeDtypeStruct(shape, dtype), in_s...  8.1 us
    all_to_all x1, starting transfers between devices, exchange(): return lax.all_to_all(blocks, axes, 0, 0, axis_index_groups=[order])  7.09 us
  transfers between devices with their start and end apart: 1, of which 1 were waited for; matrix products, arithmetic and copies ran while one was open for 0% of the time, Pallas kernels for 7%

profile of v5, /device:TPU:1, one launch (start us, length us, event | category | flops | bytes accessed | tf_op | source)
XLA Modules:
  0.0 53.4 jit_solution(6195382796356991763)
XLA Ops:
  0.0 0.8 %fusion.2.own_ref = bf16[8,128]{1,0:T(8,128)(2,1)S(1)} fusion(bf16[2,64]{1,0:T(2,128)(2,1)} %param.5, bf16[4,64]{1,0:T(4,128)(2,1)} %param.4), kind=kLoop, calls=%fused_computation.4 | loop fusion | flops 8192 | bytes 2816 | tf_op jit(solution)/shard_map/concatenate | solution.py:186
  0.8 22.6 %all_to_all.15.rows_ref = bf16[16,8,128]{2,1,0:T(8,128)(2,1)S(1)} all-to-all(bf16[16,8,128]{2,1,0:T(8,128)(2,1)S(1)} %shard_map.37), channel_id=1, replica_groups={{320,352,256,288,448,480,384,416,64,96,0,32,192,224,128,160},{321,353,2..., dimensions={0} | all-to-all | bytes 65536 | tf_op jit(solution)/shard_map/all_to_all | solution.py:29
  23.4 2.6 %shard_map.38 = bf16[32,13,2,128]{3,2,1,0:T(2,128)(2,1)S(1)} custom-call(bf16[16,8,128]{2,1,0:T(8,128)(2,1)S(1)} %all_to_all.15.rows_ref, bf16[64,32,1024]{2,1,0:T(8,128)(2,1)} %demand_in.1), custom_call_target="tpu_custom_call" | custom-call | flops 268435456 | bytes 4194304 | tf_op jit(solution)/shard_map/pallas_call | solution.py:168
  26.0 14.3 %all_to_all.16.arrived_ref = bf16[32,13,2,128]{3,2,1,0:T(2,128)(2,1)S(1)} all-to-all(bf16[32,13,2,128]{3,2,1,0:T(2,128)(2,1)S(1)} %shard_map.38), channel_id=1, replica_groups={{22,23,20,21,18,19,16,17,30,31,28,29,26,27,24,25,6,7,4,5,2,3,0,1,14,15,..., dimensions={0} | all-to-all | bytes 425984 | tf_op jit(solution)/shard_map/all_to_all | solution.py:29
  40.3 0.8 %shard_map.40 = bf16[32,16,128]{2,1,0:T(8,128)(2,1)} custom-call(bf16[32,13,2,128]{3,2,1,0:T(2,128)(2,1)S(1)} %all_to_all.16.arrived_ref), custom_call_target="tpu_custom_call" | custom-call | flops 100000 | bytes 400000 | tf_op jit(solution)/shard_map/pallas_call | solution.py:168
  41.1 7.1 %all-to-all-start.2 = ((bf16[32,16,128]{2,1,0:T(8,128)(2,1)}), bf16[32,16,128]{2,1,0:T(8,128)(2,1)S(1)}, u32[]{:S(2)}, u32[]{:S(2)}) async-start(bf16[32,16,128]{2,1,0:T(8,128)(2,1)} %shard_map.40), calls=%async_computation.2 | async-start | bytes 262144 | tf_op jit(solution)/shard_map/all_to_all | solution.py:29
  48.2 3.8 %shard_map.39.inverse_ref = bf16[192,128]{1,0:T(8,128)(2,1)S(1)} custom-call(bf16[32,13,2,128]{3,2,1,0:T(2,128)(2,1)S(1)} %all_to_all.16.arrived_ref), custom_call_target="tpu_custom_call" | custom-call | flops 16777216 | bytes 10000000 | tf_op jit(solution)/shard_map/pallas_call | solution.py:168
  52.0 0.5 all-to-all-done.2.sums_ref
  52.5 0.9 %shard_map.41 = f32[64,1024]{1,0:T(8,128)} custom-call(bf16[192,128]{1,0:T(8,128)(2,1)S(1)} %shard_map.39.inverse_ref, bf16[32,16,128]{2,1,0:T(8,128)(2,1)S(1)} %all-to-all-done.2.sums_ref), custom_call_target="tpu_custom_call" | custom-call | flops 25165824 | bytes 400000 | tf_op jit(solution)/shard_map/pallas_call | solution.py:168
  (1 shorter events, 0.0 us)
Async XLA Ops:
  41.1 11.4 %all-to-all-start.2 = ((bf16[32,16,128]{2,1,0:T(8,128)(2,1)}), bf16[32,16,128]{2,1,0:T(8,128)(2,1)S(1)}, u32[]{:S(2)}, u32[]{:S(2)}) async-start(bf16[32,16,128]{2,1,0:T(8,128)(2,1)} %shard_map.40), calls=%async_computation.2 | async-start | bytes 262144 | tf_op jit(solution)/shard_map/all_to_all | solution.py:29

commit v6 on v5

--- a/solution.py
+++ b/solution.py
@@ -9,7 +9,7 @@
 
 REST = ("hour", "cat")
 LANES = 128
-GROUP = 8
+GROUP = 4
 TALL = 16
 SUMS = 8
 HOURS = 4
@@ -43,9 +43,8 @@
     cell_n = rows_ref.shape[0]
     hours_here, cats_here, cells_here = demand_ref.shape
     depth = hours_here * cats_here
-    groups = rows_ref[...].astype(F32)
-    groups_ref[...] = groups
-    flat = groups.reshape(cell_n * GROUP, LANES)
+    flat = rows_ref[...].astype(F32).reshape(cell_n * GROUP, LANES)
+    groups_ref[...] = flat.reshape(cell_n, GROUP, LANES)
     turned = flat.T.astype(BF16)
     column = iota((cell_n * GROUP, depth), 1)
     row = iota((cell_n * GROUP, depth), 0)
@@ -59,7 +58,7 @@
     cat_cols = jnp.concatenate([cat_cols] * (depth // LANES), axis=1)
     khatri = (hour_cols * cat_cols).astype(BF16)
 
-    left_half = iota((GROUP, LANES), 1) < rank
+    left_half = iota((2 * hour_own, LANES), 1) < rank
     hour_first = lax.axis_index("cat") * (TALL // hour_own)
     hours = [groups_ref[hour_first + step][:hour_own] for step in range(TALL // hour_own)]
     over = jnp.concatenate(hours[:2], axis=0)
@@ -69,8 +68,9 @@
         share.reshape(1, HOURS, 2, LANES), (out_ref.shape[0], HOURS, 2, LANES)
     )
     cat_first = lax.axis_index("hour") * 2
-    over, under = groups_ref[cat_first], groups_ref[cat_first + 1]
-    share = jnp.where(left_half, pltpu.roll(over, rank, 1), under)[:cat_own].astype(BF16)
+    both = jnp.concatenate([groups_ref[cat_first], groups_ref[cat_first + 1]], axis=0)
+    over, under = pltpu.roll(both, rank, 1)[:cat_own], both[GROUP : GROUP + cat_own]
+    share = jnp.where(left_half[:cat_own], over, under).astype(BF16)
     out_ref[:, SUMS + HOURS] = jnp.broadcast_to(share[None], (out_ref.shape[0], 2, LANES))
 
     across = cells_here // LANES
@@ -189,8 +189,8 @@
             jnp.pad(cat_factor, ((0, GROUP - cat_own), (0, 0))),
         ],
         axis=1,
-    )
-    own = call(rows_kernel, (cell_n, GROUP, LANES), BF16, (own,), 1000, 40000)
+    ).reshape(GROUP // 2, 2, LANES)
+    own = call(rows_kernel, (cell_n,) + own.shape, BF16, (own,), 1000, 40000)
     rows = exchange(own, "cell", CELL_FIRST)
     message = call(
         functools.partial(partial_kernel, rank, hour_own, cat_own),

time: 53.7 us -> 53.4 us (level)
  no operation moved by 1% of the time
where the time goes in v6:
time: 53.4 us; the launch traced here: 53.1 us
  blocking collectives  36.8 us (69%)
  Pallas kernels  7.96 us (15%)
  starting transfers between devices  7.09 us (13%)
  other arithmetic  0.77 us (1%)
    all_to_all x2, blocking collectives, exchange(): return lax.all_to_all(blocks, axes, 0, 0, axis_index_groups=[order])  36.8 us
    pallas_call x5, Pallas kernels, call(): pl.pallas_call(kernel, out_shape=jax.ShapeDtypeStruct(shape, dtype), in_s...  7.96 us
    all_to_all x1, starting transfers between devices, exchange(): return lax.all_to_all(blocks, axes, 0, 0, axis_index_groups=[order])  7.09 us
  transfers between devices with their start and end apart: 1, of which 1 were waited for; matrix products, arithmetic and copies ran while one was open for 0% of the time, Pallas kernels for 7%

profile of v6, /device:TPU:1, one launch (start us, length us, event | category | flops | bytes accessed | tf_op | source)
XLA Modules:
  0.0 53.1 jit_solution(2652942543512834998)
XLA Ops:
  0.0 0.8 %fusion.1 = bf16[4,128]{1,0:T(4,128)(2,1)S(1)} fusion(bf16[2,64]{1,0:T(2,128)(2,1)} %param.5, bf16[4,64]{1,0:T(4,128)(2,1)} %param.4), kind=kLoop, calls=%fused_computation.2 | loop fusion | flops 3072 | bytes 1792 | tf_op jit(solution)/shard_map/concatenate | solution.py:186
  0.8 22.5 %all_to_all.15.rows_ref = bf16[16,2,2,128]{3,2,1,0:T(2,128)(2,1)S(1)} all-to-all(bf16[16,2,2,128]{3,2,1,0:T(2,128)(2,1)S(1)} %shard_map.37), channel_id=1, replica_groups={{320,352,256,288,448,480,384,416,64,96,0,32,192,224,128,160},{321,353,2..., dimensions={0} | all-to-all | bytes 32768 | tf_op jit(solution)/shard_map/all_to_all | solution.py:29
  23.3 2.5 %shard_map.38 = bf16[32,13,2,128]{3,2,1,0:T(2,128)(2,1)S(1)} custom-call(bf16[16,2,2,128]{3,2,1,0:T(2,128)(2,1)S(1)} %all_to_all.15.rows_ref, bf16[64,32,1024]{2,1,0:T(8,128)(2,1)} %demand_in.1), custom_call_target="tpu_custom_call" | custom-call | flops 268435456 | bytes 4194304 | tf_op jit(solution)/shard_map/pallas_call | solution.py:168
  25.8 14.3 %all_to_all.16.arrived_ref = bf16[32,13,2,128]{3,2,1,0:T(2,128)(2,1)S(1)} all-to-all(bf16[32,13,2,128]{3,2,1,0:T(2,128)(2,1)S(1)} %shard_map.38), channel_id=1, replica_groups={{22,23,20,21,18,19,16,17,30,31,28,29,26,27,24,25,6,7,4,5,2,3,0,1,14,15,..., dimensions={0} | all-to-all | bytes 425984 | tf_op jit(solution)/shard_map/all_to_all | solution.py:29
  40.1 0.8 %shard_map.40 = bf16[32,16,128]{2,1,0:T(8,128)(2,1)} custom-call(bf16[32,13,2,128]{3,2,1,0:T(2,128)(2,1)S(1)} %all_to_all.16.arrived_ref), custom_call_target="tpu_custom_call" | custom-call | flops 100000 | bytes 400000 | tf_op jit(solution)/shard_map/pallas_call | solution.py:168
  40.9 7.1 %all-to-all-start.2 = ((bf16[32,16,128]{2,1,0:T(8,128)(2,1)}), bf16[32,16,128]{2,1,0:T(8,128)(2,1)S(1)}, u32[]{:S(2)}, u32[]{:S(2)}) async-start(bf16[32,16,128]{2,1,0:T(8,128)(2,1)} %shard_map.40), calls=%async_computation.2 | async-start | bytes 262144 | tf_op jit(solution)/shard_map/all_to_all | solution.py:29
  48.0 3.8 %shard_map.39.inverse_ref = bf16[192,128]{1,0:T(8,128)(2,1)S(1)} custom-call(bf16[32,13,2,128]{3,2,1,0:T(2,128)(2,1)S(1)} %all_to_all.16.arrived_ref), custom_call_target="tpu_custom_call" | custom-call | flops 16777216 | bytes 10000000 | tf_op jit(solution)/shard_map/pallas_call | solution.py:168
  51.7 0.5 all-to-all-done.2.sums_ref
  52.2 0.9 %shard_map.41 = f32[64,1024]{1,0:T(8,128)} custom-call(bf16[192,128]{1,0:T(8,128)(2,1)S(1)} %shard_map.39.inverse_ref, bf16[32,16,128]{2,1,0:T(8,128)(2,1)S(1)} %all-to-all-done.2.sums_ref), custom_call_target="tpu_custom_call" | custom-call | flops 25165824 | bytes 400000 | tf_op jit(solution)/shard_map/pallas_call | solution.py:168
  (1 shorter events, 0.0 us)
Async XLA Ops:
  40.9 11.4 %all-to-all-start.2 = ((bf16[32,16,128]{2,1,0:T(8,128)(2,1)}), bf16[32,16,128]{2,1,0:T(8,128)(2,1)S(1)}, u32[]{:S(2)}, u32[]{:S(2)}) async-start(bf16[32,16,128]{2,1,0:T(8,128)(2,1)} %shard_map.40), calls=%async_computation.2 | async-start | bytes 262144 | tf_op jit(solution)/shard_map/all_to_all | solution.py:29

commit v7 on v6

--- a/solution.py
+++ b/solution.py
@@ -90,12 +90,20 @@
                 out_ref[down * across + left // LANES + over, :SUMS] = piece.reshape(SUMS, 2, LANES)
 
 
-def sum_kernel(arrived_ref, out_ref):
+def sum_kernel(arrived_ref, out_hbm, block_ref, sems):
     count = arrived_ref.shape[0]
     terms = [arrived_ref[n, :SUMS].astype(F32) for n in range(count)]
     while len(terms) > 1:
         terms = [terms[n] + terms[n + 1] for n in range(0, len(terms), 2)]
-    out_ref[...] = jnp.broadcast_to(terms[0].reshape(TALL, LANES).astype(BF16)[None], out_ref.shape)
+    block_ref[...] = jnp.broadcast_to(terms[0].reshape(TALL, LANES).astype(BF16)[None], block_ref.shape)
+    some = block_ref.shape[0]
+    copies = [
+        pltpu.make_async_copy(block_ref, out_hbm.at[pl.ds(n * some, some)], sems.at[n]) for n in range(count // some)
+    ]
+    for copy in copies:
+        copy.start()
+    for copy in copies:
+        copy.wait()
 
 
 def gram(pairs, rank):
@@ -208,7 +216,17 @@
         mib=50,
     )
     arrived = exchange(message, REST, REST_FIRST)
-    summed = call(sum_kernel, (rest_n, TALL, LANES), BF16, (arrived,), 100000, 400000)
+    summed = call(
+        sum_kernel,
+        (rest_n, TALL, LANES),
+        BF16,
+        (arrived,),
+        100000,
+        400000,
+        [pltpu.VMEM((rest_n // 4, TALL, LANES), BF16), pltpu.SemaphoreType.DMA((4,))],
+        (),
+        True,
+    )
     gathered = exchange(summed, REST, REST_FIRST)
     inverse = call(
         functools.partial(inverse_kernel, rank), (3 * rank, LANES), BF16, (arrived,), 2**24, 10**7

time: 53.4 us -> 53.4 us (level)
  no operation moved by 1% of the time
where the time goes in v7:
time: 53.4 us; the launch traced here: 53.2 us
  blocking collectives  36.8 us (69%)
  Pallas kernels  7.98 us (15%)
  starting transfers between devices  7.1 us (13%)
  other arithmetic  0.77 us (1%)
    all_to_all x2, blocking collectives, exchange(): return lax.all_to_all(blocks, axes, 0, 0, axis_index_groups=[order])  36.8 us
    pallas_call x5, Pallas kernels, call(): pl.pallas_call(kernel, out_shape=jax.ShapeDtypeStruct(shape, dtype), in_s...  7.98 us
    all_to_all x1, starting transfers between devices, exchange(): return lax.all_to_all(blocks, axes, 0, 0, axis_index_groups=[order])  7.1 us
  transfers between devices with their start and end apart: 1, of which 1 were waited for; matrix products, arithmetic and copies ran while one was open for 0% of the time, Pallas kernels for 7%

profile of v7, /device:TPU:1, one launch (start us, length us, event | category | flops | bytes accessed | tf_op | source)
XLA Modules:
  0.0 53.2 jit_solution(17165417111100324118)
XLA Ops:
  0.0 0.8 %fusion.1 = bf16[4,128]{1,0:T(4,128)(2,1)S(1)} fusion(bf16[2,64]{1,0:T(2,128)(2,1)} %param.5, bf16[4,64]{1,0:T(4,128)(2,1)} %param.4), kind=kLoop, calls=%fused_computation.2 | loop fusion | flops 3072 | bytes 1792 | tf_op jit(solution)/shard_map/concatenate | solution.py:194
  0.8 22.5 %all_to_all.15.rows_ref = bf16[16,2,2,128]{3,2,1,0:T(2,128)(2,1)S(1)} all-to-all(bf16[16,2,2,128]{3,2,1,0:T(2,128)(2,1)S(1)} %shard_map.37), channel_id=1, replica_groups={{320,352,256,288,448,480,384,416,64,96,0,32,192,224,128,160},{321,353,2..., dimensions={0} | all-to-all | bytes 32768 | tf_op jit(solution)/shard_map/all_to_all | solution.py:29
  23.3 2.5 %shard_map.38 = bf16[32,13,2,128]{3,2,1,0:T(2,128)(2,1)S(1)} custom-call(bf16[16,2,2,128]{3,2,1,0:T(2,128)(2,1)S(1)} %all_to_all.15.rows_ref, bf16[64,32,1024]{2,1,0:T(8,128)(2,1)} %demand_in.1), custom_call_target="tpu_custom_call" | custom-call | flops 268435456 | bytes 4194304 | tf_op jit(solution)/shard_map/pallas_call | solution.py:176
  25.8 14.3 %all_to_all.16.arrived_ref = bf16[32,13,2,128]{3,2,1,0:T(2,128)(2,1)S(1)} all-to-all(bf16[32,13,2,128]{3,2,1,0:T(2,128)(2,1)S(1)} %shard_map.38), channel_id=1, replica_groups={{22,23,20,21,18,19,16,17,30,31,28,29,26,27,24,25,6,7,4,5,2,3,0,1,14,15,..., dimensions={0} | all-to-all | bytes 425984 | tf_op jit(solution)/shard_map/all_to_all | solution.py:29
  40.1 0.8 %shard_map.40 = bf16[32,16,128]{2,1,0:T(8,128)(2,1)} custom-call(bf16[32,13,2,128]{3,2,1,0:T(2,128)(2,1)S(1)} %all_to_all.16.arrived_ref), custom_call_target="tpu_custom_call" | custom-call | flops 100000 | bytes 400000 | tf_op jit(solution)/shard_map/pallas_call | solution.py:176
  40.9 7.1 %all-to-all-start.2 = ((bf16[32,16,128]{2,1,0:T(8,128)(2,1)}), bf16[32,16,128]{2,1,0:T(8,128)(2,1)S(1)}, u32[]{:S(2)}, u32[]{:S(2)}) async-start(bf16[32,16,128]{2,1,0:T(8,128)(2,1)} %shard_map.40), calls=%async_computation.2 | async-start | bytes 262144 | tf_op jit(solution)/shard_map/all_to_all | solution.py:29
  48.0 3.8 %shard_map.39.inverse_ref = bf16[192,128]{1,0:T(8,128)(2,1)S(1)} custom-call(bf16[32,13,2,128]{3,2,1,0:T(2,128)(2,1)S(1)} %all_to_all.16.arrived_ref), custom_call_target="tpu_custom_call" | custom-call | flops 16777216 | bytes 10000000 | tf_op jit(solution)/shard_map/pallas_call | solution.py:176
  51.8 0.5 all-to-all-done.2.sums_ref
  52.3 0.9 %shard_map.41 = f32[64,1024]{1,0:T(8,128)} custom-call(bf16[192,128]{1,0:T(8,128)(2,1)S(1)} %shard_map.39.inverse_ref, bf16[32,16,128]{2,1,0:T(8,128)(2,1)S(1)} %all-to-all-done.2.sums_ref), custom_call_target="tpu_custom_call" | custom-call | flops 25165824 | bytes 400000 | tf_op jit(solution)/shard_map/pallas_call | solution.py:176
  (1 shorter events, 0.0 us)
Async XLA Ops:
  40.9 11.4 %all-to-all-start.2 = ((bf16[32,16,128]{2,1,0:T(8,128)(2,1)}), bf16[32,16,128]{2,1,0:T(8,128)(2,1)S(1)}, u32[]{:S(2)}, u32[]{:S(2)}) async-start(bf16[32,16,128]{2,1,0:T(8,128)(2,1)} %shard_map.40), calls=%async_computation.2 | async-start | bytes 262144 | tf_op jit(solution)/shard_map/all_to_all | solution.py:29
